TPU v7x, 128 devices: a whole 4x4x4 slice. The times are simulated.
128 devices in a mesh: ctx: 16 (over z, y_lo, core), uly: 8 (over y_hi, x).
Axes of the slice: x: 4, y: 4 (y_hi: 2, y_lo: 2; y = y_hi * 2 + y_lo), z: 4, core: 2. Of those that a mesh axis runs over, the one named last changes fastest.
Arguments:
- query_rows: bfloat16 [16384, 5120], P(('ctx', 'uly')), may hold values from -256 to 256
- key_rows: bfloat16 [2048, 5120], P(('ctx', 'uly')), may hold values from -32 to 32
- value_rows: bfloat16 [2048, 5120], P(('ctx', 'uly')), may hold values from -6 to 6
- query_tangent: bfloat16 [16384, 5120], P(('ctx', 'uly')), may hold values from -6 to 6
- key_tangent: bfloat16 [2048, 5120], P(('ctx', 'uly')), may hold values from -6 to 6
- value_tangent: bfloat16 [2048, 5120], P(('ctx', 'uly')), may hold values from -6 to 6
Outputs:
- attended: bfloat16 [16384, 5120], P(('ctx', 'uly'))
- attended_tangent: bfloat16 [16384, 5120], P(('ctx', 'uly'))
All inputs are finite; a program needn't handle non-finite values.
Results may differ from a plain program's by a relative error of at most 0.0088.
Values may be sent and summed in bfloat16 or wider, within the bound.
A program may use at most 128 MiB of HBM per device.

v0:
```python
import math

import jax
import jax.numpy as jnp
from jax import lax
from jax.sharding import PartitionSpec as P

HD = 128


def split_heads(matrix):
    return matrix.reshape(matrix.shape[0], matrix.shape[1] // HD, HD)


def split_blocks(pieces):
    piece_rows = pieces[0].shape[0]
    block_size = math.gcd(piece_rows, 256)
    return tuple(
        (
            piece.reshape(piece_rows // block_size, block_size, piece.shape[1] // HD, HD)
            for piece in pieces
        )
    )


def raw_scores(queries, key_part):
    return jnp.einsum("qhd,khd->hqk", queries, key_part, preferred_element_type=jnp.float32)


def apply_weights(weights, value_part):
    return jnp.einsum("hqk,khd->qhd", weights, value_part, preferred_element_type=jnp.float32)


def rescale(accumulated, factor):
    return accumulated * factor.T[:, :, None]


def on_device(query_rows, key_rows, value_rows, query_tangent, key_tangent, value_tangent):
    query_here, dquery_here, key_here, value_here, dkey_here, dvalue_here = (
        lax.all_to_all(query_rows, "uly", split_axis=1, concat_axis=0, tiled=True),
        lax.all_to_all(query_tangent, "uly", split_axis=1, concat_axis=0, tiled=True),
        lax.all_to_all(key_rows, "uly", split_axis=1, concat_axis=0, tiled=True),
        lax.all_to_all(value_rows, "uly", split_axis=1, concat_axis=0, tiled=True),
        lax.all_to_all(key_tangent, "uly", split_axis=1, concat_axis=0, tiled=True),
        lax.all_to_all(value_tangent, "uly", split_axis=1, concat_axis=0, tiled=True),
    )
    queries = split_heads(query_here)
    dqueries = split_heads(dquery_here)
    query_count = queries.shape[0]
    heads_here = queries.shape[1]
    score_scale = 1.0 / math.sqrt(HD)
    lowest = jnp.full((heads_here, query_count), -1e30, jnp.float32)
    zeros_rows = jnp.zeros((heads_here, query_count), jnp.float32)
    zeros_accum = jnp.zeros((query_count, heads_here, HD), jnp.float32)

    def tangent_scores(key_part, dkey_part):
        return (raw_scores(dqueries, key_part) + raw_scores(queries, dkey_part)) * score_scale

    def primal_step(running, key_block):
        running_max, row_total, accumulated = running
        key_part, value_part = key_block
        scores = raw_scores(queries, key_part) * score_scale
        new_max = jnp.maximum(running_max, jnp.max(scores, axis=-1))
        factor = jnp.exp(running_max - new_max)
        weights = jnp.exp(scores - new_max[:, :, None])
        row_total = row_total * factor + jnp.sum(weights, axis=-1)
        accumulated = rescale(accumulated, factor) + apply_weights(
            weights.astype(jnp.bfloat16), value_part
        )
        return ((new_max, row_total, accumulated), None)

    running = (lowest, zeros_rows, zeros_accum)
    running, unused = lax.scan(
        primal_step,
        running,
        split_blocks(
            (
                lax.all_gather(key_here, "ctx", axis=0, tiled=True),
                lax.all_gather(value_here, "ctx", axis=0, tiled=True),
            )
        ),
    )
    running_max, row_total, accumulated = running

    def tangent_step(running, key_block):
        moment, tangent_sum = running
        key_part, value_part, dkey_part, dvalue_part = key_block
        scores = raw_scores(queries, key_part) * score_scale
        weights = jnp.exp(scores - running_max[:, :, None])
        weights_rounded = weights.astype(jnp.bfloat16)
        weighted = weights * tangent_scores(key_part, dkey_part)
        moment = moment + jnp.sum(weighted, axis=-1)
        product_rounded = weighted.astype(jnp.bfloat16)
        tangent_sum = (
            tangent_sum
            + apply_weights(product_rounded, value_part)
            + apply_weights(weights_rounded, dvalue_part)
        )
        return ((moment, tangent_sum), None)

    running = (zeros_rows, zeros_accum)
    running, unused = lax.scan(
        tangent_step,
        running,
        split_blocks(
            (
                lax.all_gather(key_here, "ctx", axis=0, tiled=True),
                lax.all_gather(value_here, "ctx", axis=0, tiled=True),
                lax.all_gather(dkey_here, "ctx", axis=0, tiled=True),
                lax.all_gather(dvalue_here, "ctx", axis=0, tiled=True),
            )
        ),
    )
    moment, tangent_sum = running
    totals = row_total.T[:, :, None]
    mixed = accumulated / totals
    tangent = (tangent_sum - mixed * moment.T[:, :, None]) / totals
    mixed_out = mixed.astype(jnp.bfloat16).reshape(query_count, heads_here * HD)
    tangent_out = tangent.astype(jnp.bfloat16).reshape(query_count, heads_here * HD)
    return (
        lax.all_to_all(mixed_out, "uly", split_axis=0, concat_axis=1, tiled=True),
        lax.all_to_all(tangent_out, "uly", split_axis=0, concat_axis=1, tiled=True),
    )


def solution(mesh):
    placed = (
        P(("ctx", "uly"), None),
        P(("ctx", "uly"), None),
        P(("ctx", "uly"), None),
        P(("ctx", "uly"), None),
        P(("ctx", "uly"), None),
        P(("ctx", "uly"), None),
    )
    return jax.shard_map(
        on_device,
        mesh=mesh,
        in_specs=placed,
        out_specs=(P(("ctx", "uly"), None), P(("ctx", "uly"), None)),
        check_vma=False,
    )
```

profile of v0, /device:TPU:4, one launch (start us, length us, event | category | flops | bytes accessed | tf_op | source)
XLA Modules:
  0.0 450.0 jit_solution(13475247079160947695)
XLA Ops:
  8.2 13.1 %all_to_all.146 = bf16[16,8,640]{2,0,1:T(8,128)(2,1)} all-to-all(bf16[16,8,640]{2,0,1:T(8,128)(2,1)S(1)} %bitcast.169), channel_id=1, replica_groups=mesh['ctx'=16,'uly'=8] {'uly'}, dimensions={1} | all-to-all | bytes 327680 | tf_op jit(solution)/shard_map/all_to_all | solution.py:42
  22.4 11.3 %all_to_all.147 = bf16[16,8,640]{2,0,1:T(8,128)(2,1)} all-to-all(bf16[16,8,640]{2,0,1:T(8,128)(2,1)S(1)} %bitcast.170), channel_id=1, replica_groups=mesh['ctx'=16,'uly'=8] {'uly'}, dimensions={1} | all-to-all | bytes 327680 | tf_op jit(solution)/shard_map/all_to_all | solution.py:43
  34.7 11.5 %all_to_all.148 = bf16[16,8,640]{2,0,1:T(8,128)(2,1)} all-to-all(bf16[16,8,640]{2,0,1:T(8,128)(2,1)S(1)} %bitcast.171), channel_id=1, replica_groups=mesh['ctx'=16,'uly'=8] {'uly'}, dimensions={1} | all-to-all | bytes 327680 | tf_op jit(solution)/shard_map/all_to_all | solution.py:44
  59.3 6.0 %all-to-all-start.1 = ((bf16[128,8,640]{0,2,1:T(8,128)(2,1)}), bf16[128,8,640]{0,2,1:T(8,128)(2,1)S(1)}, u32[]{:S(2)}, u32[]{:S(2)}) async-start(bf16[128,8,640]{0,2,1:T(8,128)(2,1)} %bitcast.2), calls=%async_computation.1 | async-start | bytes 2621440 | tf_op jit(solution)/shard_map/all_to_all | solution.py:40
  66.7 14.6 %all-to-all-done.1 = bf16[128,8,640]{0,2,1:T(8,128)(2,1)S(1)} async-done(((bf16[128,8,640]{0,2,1:T(8,128)(2,1)}), bf16[128,8,640]{0,2,1:T(8,128)(2,1)S(1)}, u32[]{:S(2)}, u32[]{:S(2)}) %all-to-all-start.1) | async-done | bytes 1310752 | tf_op jit(solution)/shard_map/all_to_all | solution.py:40
  93.8 11.6 %all-to-all-done.4 = bf16[128,8,640]{0,2,1:T(8,128)(2,1)S(1)} async-done(((bf16[128,8,640]{0,2,1:T(8,128)(2,1)}), bf16[128,8,640]{0,2,1:T(8,128)(2,1)S(1)}, u32[]{:S(2)}, u32[]{:S(2)}) %all-to-all-start.4) | async-done | bytes 1310752 | tf_op jit(solution)/shard_map/all_to_all | solution.py:41
  112.3 7.0 %reshape.67 = bf16[8,256,5,128]{3,2,1,0:T(8,128)(2,1)} reshape(bf16[2048,640]{1,0:T(8,128)(2,1)} %all-gather.5.cloned.1.call-done) | data formatting | bytes 5242880 | tf_op jit(solution)/shard_map/reshape | solution.py:20
  123.8 7.0 %reshape.68 = bf16[8,256,5,128]{3,2,1,0:T(8,128)(2,1)} reshape(bf16[2048,640]{1,0:T(8,128)(2,1)} %all-gather.7.cloned.1.call-done) | data formatting | bytes 5242880 | tf_op jit(solution)/shard_map/reshape | solution.py:20
  130.8 6.2 %copy.89 = bf16[8,256,5,128]{1,3,2,0:T(8,128)(2,1)} copy(bf16[8,256,5,128]{3,2,1,0:T(8,128)(2,1)} %reshape.68) | data formatting | bytes 5242880
  137.0 91.2 %while.28 = (s32[]{:T(128)}, f32[5,1024]{1,0:T(8,128)S(1)}, f32[5,1024]{1,0:T(8,128)S(1)}, f32[1024,5,128]{0,2,1:T(8,128)}, bf16[8,256,5,128]{3,1,2,0:T(8,128)(2...) while((s32[]{:T(128)}, f32[5,1024]{1,0:T(8,128)S(1)}, ...), condition=%wide.region_3.4_spmd.clone, body=%wide.region_0.3_spmd.clone.sunk | while | flops 683571200 | bytes 38995096 | solution.py:73
  151.9 6.4 %bitcast_add_fusion.5 = f32[1024,5,128]{0,2,1:T(8,128)} fusion(f32[1024,5,128]{0,2,1:T(8,128)} %get-tuple-element.398, f32[5,256,1024]{2,1,0:T(8,128)} %get-tuple-element.372, f32[5,1024]{1,0:T(8,128)S(1)} %get-tuple-element.405, f32[1024,5]{0,1:T(8,128)S(1)} %get-tuple-element.373, pred[]{:T(512)S(6)} %compare.6, ...), kind=kOutput, calls=%fused_computation.6.clone.1 | convolution fusion | flops 341442560 | bytes 10854913 | tf_op jit(solution)/shard_map/while/body/eval_jaxpr/hqk,khd->qhd/dot_general | solution.py:31
  163.4 6.4 %bitcast_add_fusion.5 = f32[1024,5,128]{0,2,1:T(8,128)} fusion(f32[1024,5,128]{0,2,1:T(8,128)} %get-tuple-element.398, f32[5,256,1024]{2,1,0:T(8,128)} %get-tuple-element.372, f32[5,1024]{1,0:T(8,128)S(1)} %get-tuple-element.405, f32[1024,5]{0,1:T(8,128)S(1)} %get-tuple-element.373, pred[]{:T(512)S(6)} %compare.6, ...), kind=kOutput, calls=%fused_computation.6.clone.1 | convolution fusion | flops 341442560 | bytes 10854913 | tf_op jit(solution)/shard_map/while/body/eval_jaxpr/hqk,khd->qhd/dot_general | solution.py:31
  174.9 6.5 %bitcast_add_fusion.5 = f32[1024,5,128]{0,2,1:T(8,128)} fusion(f32[1024,5,128]{0,2,1:T(8,128)} %get-tuple-element.398, f32[5,256,1024]{2,1,0:T(8,128)} %get-tuple-element.372, f32[5,1024]{1,0:T(8,128)S(1)} %get-tuple-element.405, f32[1024,5]{0,1:T(8,128)S(1)} %get-tuple-element.373, pred[]{:T(512)S(6)} %compare.6, ...), kind=kOutput, calls=%fused_computation.6.clone.1 | convolution fusion | flops 341442560 | bytes 10854913 | tf_op jit(solution)/shard_map/while/body/eval_jaxpr/hqk,khd->qhd/dot_general | solution.py:31
  186.5 6.4 %bitcast_add_fusion.5 = f32[1024,5,128]{0,2,1:T(8,128)} fusion(f32[1024,5,128]{0,2,1:T(8,128)} %get-tuple-element.398, f32[5,256,1024]{2,1,0:T(8,128)} %get-tuple-element.372, f32[5,1024]{1,0:T(8,128)S(1)} %get-tuple-element.405, f32[1024,5]{0,1:T(8,128)S(1)} %get-tuple-element.373, pred[]{:T(512)S(6)} %compare.6, ...), kind=kOutput, calls=%fused_computation.6.clone.1 | convolution fusion | flops 341442560 | bytes 10854913 | tf_op jit(solution)/shard_map/while/body/eval_jaxpr/hqk,khd->qhd/dot_general | solution.py:31
  197.9 6.4 %bitcast_add_fusion.5 = f32[1024,5,128]{0,2,1:T(8,128)} fusion(f32[1024,5,128]{0,2,1:T(8,128)} %get-tuple-element.398, f32[5,256,1024]{2,1,0:T(8,128)} %get-tuple-element.372, f32[5,1024]{1,0:T(8,128)S(1)} %get-tuple-element.405, f32[1024,5]{0,1:T(8,128)S(1)} %get-tuple-element.373, pred[]{:T(512)S(6)} %compare.6, ...), kind=kOutput, calls=%fused_computation.6.clone.1 | convolution fusion | flops 341442560 | bytes 10854913 | tf_op jit(solution)/shard_map/while/body/eval_jaxpr/hqk,khd->qhd/dot_general | solution.py:31
  209.4 6.4 %bitcast_add_fusion.5 = f32[1024,5,128]{0,2,1:T(8,128)} fusion(f32[1024,5,128]{0,2,1:T(8,128)} %get-tuple-element.398, f32[5,256,1024]{2,1,0:T(8,128)} %get-tuple-element.372, f32[5,1024]{1,0:T(8,128)S(1)} %get-tuple-element.405, f32[1024,5]{0,1:T(8,128)S(1)} %get-tuple-element.373, pred[]{:T(512)S(6)} %compare.6, ...), kind=kOutput, calls=%fused_computation.6.clone.1 | convolution fusion | flops 341442560 | bytes 10854913 | tf_op jit(solution)/shard_map/while/body/eval_jaxpr/hqk,khd->qhd/dot_general | solution.py:31
  220.9 6.4 %bitcast_add_fusion.5 = f32[1024,5,128]{0,2,1:T(8,128)} fusion(f32[1024,5,128]{0,2,1:T(8,128)} %get-tuple-element.398, f32[5,256,1024]{2,1,0:T(8,128)} %get-tuple-element.372, f32[5,1024]{1,0:T(8,128)S(1)} %get-tuple-element.405, f32[1024,5]{0,1:T(8,128)S(1)} %get-tuple-element.373, pred[]{:T(512)S(6)} %compare.6, ...), kind=kOutput, calls=%fused_computation.6.clone.1 | convolution fusion | flops 341442560 | bytes 10854913 | tf_op jit(solution)/shard_map/while/body/eval_jaxpr/hqk,khd->qhd/dot_general | solution.py:31
  228.3 7.0 %reshape.65 = bf16[8,256,5,128]{3,2,1,0:T(8,128)(2,1)} reshape(bf16[2048,640]{1,0:T(8,128)(2,1)} %all-gather.9.cloned.1.call-done) | data formatting | bytes 5242880 | tf_op jit(solution)/shard_map/reshape | solution.py:20
  239.8 7.0 %reshape.66 = bf16[8,256,5,128]{3,2,1,0:T(8,128)(2,1)} reshape(bf16[2048,640]{1,0:T(8,128)(2,1)} %all-gather.11.cloned.1.call-done) | data formatting | bytes 5242880 | tf_op jit(solution)/shard_map/reshape | solution.py:20
  246.7 6.2 %copy.103 = bf16[8,256,5,128]{1,3,2,0:T(8,128)(2,1)} copy(bf16[8,256,5,128]{3,2,1,0:T(8,128)(2,1)} %reshape.66) | data formatting | bytes 5242880
  252.9 136.1 %while.29 = (s32[]{:T(128)}, f32[5,1024]{1,0:T(8,128)S(1)}, f32[1024,5,128]{0,2,1:T(8,128)}, bf16[8,256,5,128]{3,1,2,0:T(8,128)(2,1)}, bf16[1024,5,128]{2,0,1:T(...) while((s32[]{:T(128)}, f32[5,1024]{1,0:T(8,128)S(1)}, ...), condition=%wide.region_6.7_spmd.clone, body=%wide.region_4.6_spmd.clone.sunk | while | flops 1692800000 | bytes 47639164 | solution.py:102
  404.7 12.9 %all-to-all-done.3 = bf16[8,128,640]{2,1,0:T(8,128)(2,1)S(1)} async-done(((bf16[8,128,640]{2,1,0:T(8,128)(2,1)}), bf16[8,128,640]{2,1,0:T(8,128)(2,1)S(1)}, u32[]{:S(2)}, u32[]{:S(2)}) %all-to-all-start.3) | async-done | bytes 1310752 | tf_op jit(solution)/shard_map/all_to_all | solution.py:121
  417.7 6.2 %all-to-all-start.7 = ((bf16[8,128,640]{2,1,0:T(8,128)(2,1)}), bf16[8,128,640]{2,1,0:T(8,128)(2,1)S(1)}, u32[]{:S(2)}, u32[]{:S(2)}) async-start(bf16[8,128,640]{2,1,0:T(8,128)(2,1)} %copy.104), calls=%async_computation.7 | async-start | bytes 2621440 | tf_op jit(solution)/shard_map/all_to_all | solution.py:122
  427.7 13.6 %all-to-all-done.7 = bf16[8,128,640]{2,1,0:T(8,128)(2,1)S(1)} async-done(((bf16[8,128,640]{2,1,0:T(8,128)(2,1)}), bf16[8,128,640]{2,1,0:T(8,128)(2,1)S(1)}, u32[]{:S(2)}, u32[]{:S(2)}) %all-to-all-start.7) | async-done | bytes 1310752 | tf_op jit(solution)/shard_map/all_to_all | solution.py:122
  (179 shorter events, 249.6 us)
Async XLA Ops:
  7.2 46.3 %copy-start = (bf16[128,5120]{1,0:T(8,128)(2,1)S(1)}, bf16[128,5120]{1,0:T(8,128)(2,1)}, u32[]{:S(2)}) copy-start(bf16[128,5120]{1,0:T(8,128)(2,1)} %param.10) | copy-start | bytes 3932164
  7.2 105.2 %all-gather.5.cloned.1.call-start = ((), (), s32[]{:S(2)}) async-start(), calls=%async_computation.8 | async-start | bytes 2785280 | tf_op jit(solution)/shard_map/all_gather | solution.py:78
  21.4 102.4 %all-gather.7.cloned.1.call-start = ((), (), s32[]{:S(2)}) async-start(), calls=%async_computation.9 | async-start | bytes 2785280 | tf_op jit(solution)/shard_map/all_gather | solution.py:79
  33.7 194.6 %all-gather.9.cloned.1.call-start = ((), (), s32[]{:S(2)}) async-start(), calls=%async_computation.10 | async-start | bytes 2785280 | tf_op jit(solution)/shard_map/all_gather | solution.py:109
  47.8 11.5 %all-to-all-start.6 = ((bf16[16,8,640]{2,0,1:T(8,128)(2,1)}), bf16[16,8,640]{2,0,1:T(8,128)(2,1)S(1)}, u32[]{:S(2)}, u32[]{:S(2)}) async-start(bf16[16,8,640]{2,0,1:T(8,128)(2,1)} %bitcast.109), calls=%async_computation.6 | async-start | bytes 327680 | tf_op jit(solution)/shard_map/all_to_all | solution.py:45
  53.5 11.8 %copy-start.1 = (bf16[128,5120]{1,0:T(8,128)(2,1)S(1)}, bf16[128,5120]{1,0:T(8,128)(2,1)}, u32[]{:S(2)}) copy-start(bf16[128,5120]{1,0:T(8,128)(2,1)} %param.13) | copy-start | bytes 3932164
  59.3 7.4 %copy-start.2 = (bf16[16,8,640]{2,0,1:T(8,128)(2,1)}, bf16[16,8,640]{2,0,1:T(8,128)(2,1)S(1)}, u32[]{:S(2)}) copy-start(bf16[16,8,640]{2,0,1:T(8,128)(2,1)S(1)} %all-to-all-done.6) | copy-start | bytes 491524
  59.3 22.0 %all-to-all-start.1 = ((bf16[128,8,640]{0,2,1:T(8,128)(2,1)}), bf16[128,8,640]{0,2,1:T(8,128)(2,1)S(1)}, u32[]{:S(2)}, u32[]{:S(2)}) async-start(bf16[128,8,640]{0,2,1:T(8,128)(2,1)} %bitcast.2), calls=%async_computation.1 | async-start | bytes 2621440 | tf_op jit(solution)/shard_map/all_to_all | solution.py:40
  81.3 24.1 %all-to-all-start.4 = ((bf16[128,8,640]{0,2,1:T(8,128)(2,1)}), bf16[128,8,640]{0,2,1:T(8,128)(2,1)S(1)}, u32[]{:S(2)}, u32[]{:S(2)}) async-start(bf16[128,8,640]{0,2,1:T(8,128)(2,1)} %bitcast.9), calls=%async_computation.4 | async-start | bytes 2621440 | tf_op jit(solution)/shard_map/all_to_all | solution.py:41
  86.3 153.4 %all-gather.11.cloned.1.call-start = ((), (), s32[]{:S(2)}) async-start(), calls=%async_computation.11 | async-start | bytes 2785280 | tf_op jit(solution)/shard_map/all_gather | solution.py:110
  151.8 6.4 %slice-start = ((s8[5242880]{0:T(1024)(128)(4,1)}), s8[4194304]{0:T(1024)(128)(4,1)S(1)}, s32[]{:S(2)}) async-start(s8[5242880]{0:T(1024)(128)(4,1)} %bitcast.153), calls=%async_computation.12 | async-start | bytes 8388608 | tf_op jit(solution)/shard_map/while
  151.9 6.4 %slice-start.1 = ((s8[5242880]{0:T(1024)(128)(4,1)}), s8[1048576]{0:T(1024)(128)(4,1)S(1)}, s32[]{:S(2)}) async-start(s8[5242880]{0:T(1024)(128)(4,1)} %bitcast.153), calls=%async_computation.13 | async-start | bytes 2097152 | tf_op jit(solution)/shard_map/while
  163.3 6.5 %slice-start = ((s8[5242880]{0:T(1024)(128)(4,1)}), s8[4194304]{0:T(1024)(128)(4,1)S(1)}, s32[]{:S(2)}) async-start(s8[5242880]{0:T(1024)(128)(4,1)} %bitcast.153), calls=%async_computation.12 | async-start | bytes 8388608 | tf_op jit(solution)/shard_map/while
  163.3 6.4 %slice-start.1 = ((s8[5242880]{0:T(1024)(128)(4,1)}), s8[1048576]{0:T(1024)(128)(4,1)S(1)}, s32[]{:S(2)}) async-start(s8[5242880]{0:T(1024)(128)(4,1)} %bitcast.153), calls=%async_computation.13 | async-start | bytes 2097152 | tf_op jit(solution)/shard_map/while
  174.8 6.5 %slice-start = ((s8[5242880]{0:T(1024)(128)(4,1)}), s8[4194304]{0:T(1024)(128)(4,1)S(1)}, s32[]{:S(2)}) async-start(s8[5242880]{0:T(1024)(128)(4,1)} %bitcast.153), calls=%async_computation.12 | async-start | bytes 8388608 | tf_op jit(solution)/shard_map/while
  174.9 6.5 %slice-start.1 = ((s8[5242880]{0:T(1024)(128)(4,1)}), s8[1048576]{0:T(1024)(128)(4,1)S(1)}, s32[]{:S(2)}) async-start(s8[5242880]{0:T(1024)(128)(4,1)} %bitcast.153), calls=%async_computation.13 | async-start | bytes 2097152 | tf_op jit(solution)/shard_map/while
  186.4 6.4 %slice-start = ((s8[5242880]{0:T(1024)(128)(4,1)}), s8[4194304]{0:T(1024)(128)(4,1)S(1)}, s32[]{:S(2)}) async-start(s8[5242880]{0:T(1024)(128)(4,1)} %bitcast.153), calls=%async_computation.12 | async-start | bytes 8388608 | tf_op jit(solution)/shard_map/while
  197.9 6.4 %slice-start = ((s8[5242880]{0:T(1024)(128)(4,1)}), s8[4194304]{0:T(1024)(128)(4,1)S(1)}, s32[]{:S(2)}) async-start(s8[5242880]{0:T(1024)(128)(4,1)} %bitcast.153), calls=%async_computation.12 | async-start | bytes 8388608 | tf_op jit(solution)/shard_map/while
  197.9 6.4 %slice-start.1 = ((s8[5242880]{0:T(1024)(128)(4,1)}), s8[1048576]{0:T(1024)(128)(4,1)S(1)}, s32[]{:S(2)}) async-start(s8[5242880]{0:T(1024)(128)(4,1)} %bitcast.153), calls=%async_computation.13 | async-start | bytes 2097152 | tf_op jit(solution)/shard_map/while
  209.4 6.4 %slice-start = ((s8[5242880]{0:T(1024)(128)(4,1)}), s8[4194304]{0:T(1024)(128)(4,1)S(1)}, s32[]{:S(2)}) async-start(s8[5242880]{0:T(1024)(128)(4,1)} %bitcast.153), calls=%async_computation.12 | async-start | bytes 8388608 | tf_op jit(solution)/shard_map/while
  220.9 6.4 %slice-start = ((s8[5242880]{0:T(1024)(128)(4,1)}), s8[4194304]{0:T(1024)(128)(4,1)S(1)}, s32[]{:S(2)}) async-start(s8[5242880]{0:T(1024)(128)(4,1)} %bitcast.153), calls=%async_computation.12 | async-start | bytes 8388608 | tf_op jit(solution)/shard_map/while
  220.9 6.4 %slice-start.1 = ((s8[5242880]{0:T(1024)(128)(4,1)}), s8[1048576]{0:T(1024)(128)(4,1)S(1)}, s32[]{:S(2)}) async-start(s8[5242880]{0:T(1024)(128)(4,1)} %bitcast.153), calls=%async_computation.13 | async-start | bytes 2097152 | tf_op jit(solution)/shard_map/while
  395.8 21.9 %all-to-all-start.3 = ((bf16[8,128,640]{2,1,0:T(8,128)(2,1)}), bf16[8,128,640]{2,1,0:T(8,128)(2,1)S(1)}, u32[]{:S(2)}, u32[]{:S(2)}) async-start(bf16[8,128,640]{2,1,0:T(8,128)(2,1)} %copy.90), calls=%async_computation.3 | async-start | bytes 2621440 | tf_op jit(solution)/shard_map/all_to_all | solution.py:121
  417.7 23.6 %all-to-all-start.7 = ((bf16[8,128,640]{2,1,0:T(8,128)(2,1)}), bf16[8,128,640]{2,1,0:T(8,128)(2,1)S(1)}, u32[]{:S(2)}, u32[]{:S(2)}) async-start(bf16[8,128,640]{2,1,0:T(8,128)(2,1)} %copy.104), calls=%async_computation.7 | async-start | bytes 2621440 | tf_op jit(solution)/shard_map/all_to_all | solution.py:122
  (4 other events, 24.1 us)
Sparse Core Ops, SparseCore 0:
  21.5 36.4 all-gather.4
  59.7 48.3 all-gather.6
  109.8 37.9 all-gather.8
  149.4 35.0 all-gather.10
where the time goes:
time: 456 us; the launch traced here: 450 us
  matrix products  219 us (48%)
  local copies, waits for them, and re-layouts  82.7 us (18%)
  waiting for transfers between devices  57.7 us (13%)
  blocking collectives  35.9 us (8%)
  starting transfers between devices  28.2 us (6%)
  between operations  13.9 us (3%)
  other arithmetic  11.9 us (3%)
    dot_general x24, matrix products, apply_weights(): jnp.einsum('hqk,khd->qhd', weights, value_part, preferred_element_type=jn...  123 us
    dot_general x32, matrix products, raw_scores(): jnp.einsum('qhd,khd->hqk', queries, key_part, preferred_element_type=jnp....  96.3 us
    unnamed x18, local copies, waits for them, and re-layouts  33.6 us
    reshape x4, local copies, waits for them, and re-layouts, split_blocks(): piece.reshape(piece_rows // block_size, block_size, piece.shape[1] // HD,...  28 us
    all_to_all x1, waiting for transfers between devices, on_device(): lax.all_to_all(query_rows, 'uly', split_axis=1, concat_axis=0, tiled=True)  14.6 us
    all_to_all x1, waiting for transfers between devices, on_device(): lax.all_to_all(tangent_out, 'uly', split_axis=0, concat_axis=1, tiled=True)  13.6 us
    all_to_all x1, blocking collectives, on_device(): lax.all_to_all(key_rows, 'uly', split_axis=1, concat_axis=0, tiled=True)  13.1 us
    all_to_all x1, waiting for transfers between devices, on_device(): lax.all_to_all(mixed_out, 'uly', split_axis=0, concat_axis=1, tiled=True)  12.9 us
  transfers between devices with their start and end apart: 9, of which 5 were waited for; matrix products, arithmetic and copies ran while one was open for 34% of the time, Pallas kernels for 0%

commit v1 on v0

v1 whole, which is shorter than its diff:
```python
import functools
import math

import jax
import jax.numpy as jnp
from jax import lax
from jax.experimental import pallas as pl
from jax.experimental.pallas import tpu as pltpu
from jax.sharding import PartitionSpec as P

HD = 128
SLOTS = 5
GROUP = 8
QROWS = 128
KROWS = 16
BLOCK = GROUP * KROWS
QUERIES = GROUP * QROWS
KEYS = 2048
COLS = 5120
TILE = 256
SCALE = 1.0 / math.sqrt(HD)
SCALE_LOG2 = SCALE * math.log2(math.e)
MESH = pl.DeviceIdType.MESH

LAYOUT = ((0, 1, 2, 0),) * SLOTS


def scores_of(left, right):
    return lax.dot_general(left, right, (((1,), (1,)), ((), ())), preferred_element_type=jnp.float32)


def mix(left, right):
    return jnp.dot(left, right, preferred_element_type=jnp.float32)


class Place:
    def __init__(self, slot, xyz, core):
        ring, pair, keys, shift = LAYOUT[slot]
        self.order, self.shift, self.core, self.slot = (ring, pair, keys), shift, core, slot
        self.a = xyz[ring]
        self.b = lax.rem(xyz[pair] + shift, 4)
        self.c = xyz[keys]
        self.member = self.a + 4 * lax.rem(self.b, 2)
        self.kind = self.kind_of(self.a, self.b)
        self.block = self.block_of(self.b, self.c, core)

    def kind_of(self, a, b):
        return a + 4 * lax.rem(lax.rem(b, 2) + lax.div(b, 2), 2)

    def block_of(self, b, c, core):
        return (c * 2 + lax.div(b, 2)) * 2 + core

    def device(self, a, b, c, core):
        xyz = [None] * 3
        for axis, at in zip(self.order, (a, lax.rem(b + 4 - self.shift, 4), c)):
            xyz[axis] = at
        x, y, z = xyz
        return (z * 4 + lax.rem(y, 2) * 2 + core, lax.div(y, 2) * 4 + x)

    def peers(self):
        found = []
        for da in range(4):
            for db in range(2):
                if da or db:
                    a = lax.rem(self.a + da, 4)
                    b = self.b + (1 - 2 * lax.rem(self.b, 2)) * db
                    found.append((self.device(a, b, self.c, self.core), a + 4 * lax.rem(b, 2), self.kind_of(a, b)))
        return found

    def across(self):
        return self.device(self.a, 3 - self.b, self.c, self.core)

    def along(self, step):
        return self.device(self.a, self.b, lax.rem(self.c + step, 4), self.core)

    def twin(self):
        return self.device(self.a, self.b, self.c, 1 - self.core)


def columns(head):
    return pl.ds(pl.multiple_of(head * HD, HD), HD)


def rows(start, size):
    return pl.ds(pl.multiple_of(start, 16), size)


def send(src, dst, send_sem, recv_sem, device):
    pltpu.make_async_remote_copy(
        src_ref=src, dst_ref=dst, send_sem=send_sem, recv_sem=recv_sem, device_id=device, device_id_type=MESH
    ).start()


def wait_bytes(ref, sem):
    pltpu.make_async_copy(ref, ref, sem).wait()


def kernel(
    q_ref, k_ref, v_ref, dq_ref, dk_ref, dv_ref, out_ref,
    q_own, k_own, q_all, k_all, o_all,
    stage_sem, q_send, q_recv, k1_send, k1_recv, k2_send, across_recv, along_recv, twin_recv, o_send, o_recv,
):
    ctx, uly = lax.axis_index("ctx"), lax.axis_index("uly")
    core = lax.rem(ctx, 2)
    xyz = (lax.rem(uly, 4), lax.div(uly, 4) * 2 + lax.rem(lax.div(ctx, 2), 2), lax.div(ctx, 4))
    places = [Place(slot, xyz, core) for slot in range(SLOTS)]

    staged = [
        pltpu.make_async_copy(ref, k_own.at[at], stage_sem.at[at]) for at, ref in enumerate((k_ref, dk_ref, v_ref, dv_ref))
    ] + [pltpu.make_async_copy(ref, q_own.at[at], stage_sem.at[4 + at]) for at, ref in enumerate((q_ref, dq_ref))]
    for copy in staged:
        copy.start()

    barrier = pltpu.get_barrier_semaphore()
    partners = [places[0].twin()]
    for slot, place in enumerate(places):
        if LAYOUT[slot] not in LAYOUT[:slot]:
            partners += [device for device, _, _ in place.peers()]
            partners += [place.across()] + [place.along(step) for step in (1, 2, 3)]
    for device in partners:
        pl.semaphore_signal(barrier, inc=1, device_id=device, device_id_type=MESH)
    pl.semaphore_wait(barrier, len(partners))
    for copy in staged:
        copy.wait()

    def send_keys(slot):
        place = places[slot]
        there = k_all.at[slot, :, rows(place.block * BLOCK + place.member * KROWS, KROWS), :]
        for device, _, kind in place.peers():
            send(k_own.at[:, :, columns(slot * GROUP + kind)], there, k1_send.at[slot], k1_recv.at[slot], device)
        pltpu.make_async_copy(k_own.at[:, :, columns(slot * GROUP + place.kind)], there, k1_recv.at[slot]).start()

    def send_queries(slot):
        place = places[slot]
        there = q_all.at[slot, :, rows(place.member * QROWS, QROWS), :]
        for device, _, kind in place.peers():
            send(q_own.at[:, :, columns(slot * GROUP + kind)], there, q_send.at[slot], q_recv.at[slot], device)
        pltpu.make_async_copy(q_own.at[:, :, columns(slot * GROUP + place.kind)], there, q_recv.at[slot]).start()

    def block_ref(slot, block):
        return k_all.at[slot, :, rows(block * BLOCK, BLOCK), :]

    def to_twin(slot, block):
        ref = block_ref(slot, block)
        send(ref, ref, k2_send.at[slot], twin_recv.at[slot], places[slot].twin())

    def along_all(slot, block, which):
        ref = block_ref(slot, block)
        for step in (1, 3, 2):
            send(ref, ref, k2_send.at[slot], along_recv.at[slot, which, step - 1], places[slot].along(step))
        to_twin(slot, block)

    def own_block(slot):
        place = places[slot]
        ref = block_ref(slot, place.block)
        wait_bytes(ref, k1_recv.at[slot])
        send(ref, ref, k2_send.at[slot], across_recv.at[slot], place.across())
        along_all(slot, place.block, 0)

    def across_block(slot):
        place = places[slot]
        block = place.block_of(3 - place.b, place.c, core)
        wait_bytes(block_ref(slot, block), across_recv.at[slot])
        along_all(slot, block, 1)

    def along_blocks(slot, which):
        place = places[slot]
        b = 3 - place.b if which else place.b
        for step in (1, 3, 2):
            block = place.block_of(b, lax.rem(place.c + 4 - step, 4), core)
            wait_bytes(block_ref(slot, block), along_recv.at[slot, which, step - 1])
            to_twin(slot, block)

    def attend(slot):
        def tile(at, _):
            here = rows(at * TILE, TILE)
            query, dquery = q_all[slot, 0, here, :], q_all[slot, 1, here, :]
            key, dkey = k_all[slot, 0], k_all[slot, 1]
            value, dvalue = k_all[slot, 2], k_all[slot, 3]
            scores = scores_of(query, key) * SCALE_LOG2
            tangents = scores_of(jnp.concatenate([dquery, query], 1), jnp.concatenate([key, dkey], 1))
            highest = jnp.max(scores, axis=1, keepdims=True)
            weights = jnp.exp2(scores - highest)
            total = jnp.sum(weights, axis=1, keepdims=True)
            weights_rounded = weights.astype(jnp.bfloat16)
            product = weights * (tangents * SCALE)
            moment = jnp.sum(product, axis=1, keepdims=True)
            both = mix(weights_rounded, jnp.concatenate([value, dvalue], 1))
            mixed = both[:, :HD] / total
            tangent = (mix(product.astype(jnp.bfloat16), value) + both[:, HD:] - mixed * moment) / total
            o_all[slot, 0, here, :] = mixed.astype(jnp.bfloat16)
            o_all[slot, 1, here, :] = tangent.astype(jnp.bfloat16)
            return 0

        lax.fori_loop(0, QUERIES // TILE, tile, 0)

    def send_outputs(slot):
        place = places[slot]
        there = out_ref.at[:, :, columns(slot * GROUP + place.kind)]
        for device, member, _ in place.peers():
            send(o_all.at[slot, :, rows(member * QROWS, QROWS), :], there, o_send.at[slot], o_recv, device)
        pltpu.make_async_copy(o_all.at[slot, :, rows(place.member * QROWS, QROWS), :], there, o_recv).start()

    for slot in range(SLOTS):
        send_keys(slot)
    send_queries(0)
    own_block(0)
    across_block(0)
    send_queries(1)
    own_block(1)
    along_blocks(0, 0)
    along_blocks(0, 1)
    for slot in range(SLOTS):
        if slot + 1 < SLOTS:
            across_block(slot + 1)
        if slot + 2 < SLOTS:
            send_queries(slot + 2)
            own_block(slot + 2)
        wait_bytes(k_all.at[slot, :, : KEYS // 2, :], twin_recv.at[slot])
        wait_bytes(q_all.at[slot], q_recv.at[slot])
        attend(slot)
        send_outputs(slot)
        if slot + 1 < SLOTS:
            along_blocks(slot + 1, 0)
            along_blocks(slot + 1, 1)

    for slot in range(SLOTS):
        wait_bytes(k_all.at[slot, :, : 7 * KROWS, :], k1_send.at[slot])
        wait_bytes(q_all.at[slot, :, : 7 * QROWS, :], q_send.at[slot])
        wait_bytes(k_all.at[slot, :, : 15 * BLOCK, :], k2_send.at[slot])
        wait_bytes(o_all.at[slot, :, : 7 * QROWS, :], o_send.at[slot])
    wait_bytes(out_ref, o_recv)


def on_device(query_rows, key_rows, value_rows, query_tangent, key_tangent, value_tangent):
    dma = pltpu.SemaphoreType.DMA
    out = pl.pallas_call(
        kernel,
        out_shape=jax.ShapeDtypeStruct((2, QROWS, COLS), jnp.bfloat16),
        in_specs=[pl.BlockSpec(memory_space=pl.ANY)] * 6,
        out_specs=pl.BlockSpec(memory_space=pl.ANY),
        scratch_shapes=[
            pltpu.VMEM((2, QROWS, COLS), jnp.bfloat16),
            pltpu.VMEM((4, KROWS, COLS), jnp.bfloat16),
            pltpu.VMEM((SLOTS, 2, QUERIES, HD), jnp.bfloat16),
            pltpu.VMEM((SLOTS, 4, KEYS, HD), jnp.bfloat16),
            pltpu.VMEM((SLOTS, 2, QUERIES, HD), jnp.bfloat16),
            dma((6,)),
            dma((SLOTS,)),
            dma((SLOTS,)),
            dma((SLOTS,)),
            dma((SLOTS,)),
            dma((SLOTS,)),
            dma((SLOTS,)),
            dma((SLOTS, 2, 3)),
            dma((SLOTS,)),
            dma((SLOTS,)),
            dma(()),
        ],
        compiler_params=pltpu.CompilerParams(collective_id=0, has_side_effects=True, vmem_limit_bytes=56 * 2**20),
        cost_estimate=pl.CostEstimate(flops=16_000_000_000, bytes_accessed=6_000_000, transcendentals=10_500_000),
        name="tangent_attention",
    )(query_rows, key_rows, value_rows, query_tangent, key_tangent, value_tangent)
    return out[0], out[1]


def solution(mesh):
    whole = P(("ctx", "uly"), None)
    return jax.shard_map(on_device, mesh=mesh, in_specs=(whole,) * 6, out_specs=(whole, whole), check_vma=False)
```

time: 456 us -> 91.1 us (0.20); the launches traced: 450 us -> 90.1 us
  matrix products: 219 us -> 0 us
  Pallas kernels: 0 us -> 86.1 us
  local copies, waits for them, and re-layouts: 82.7 us -> 3.37 us
  waiting for transfers between devices: 57.7 us -> 0 us
  blocking collectives: 35.9 us -> 0 us
  starting transfers between devices: 28.2 us -> 0 us
  between operations: 13.9 us -> 0.64 us
  other arithmetic: 11.9 us -> 0 us
    dot_general x56 -> x0, matrix products: 219 us -> none  [the longest x24 123 us: apply_weights(): jnp.einsum('hqk,khd->qhd', weights, value_part, preferred_element_type=jn...]
    pallas_call x0 -> x1, Pallas kernels: none -> 86.1 us  [on_device(): pl.pallas_call(kernel, out_shape=jax.ShapeDtypeStruct((2, QROWS, COLS), j...]
    all_to_all x5 -> x0, waiting for transfers between devices: 57 us -> none  [the longest x1 14.6 us: on_device(): lax.all_to_all(query_rows, 'uly', split_axis=1, concat_axis=0, tiled=True)]
    all_to_all x3 -> x0, blocking collectives: 35.9 us -> none  [the longest x1 13.1 us: on_device(): lax.all_to_all(key_rows, 'uly', split_axis=1, concat_axis=0, tiled=True)]
    reshape x6 -> x0, local copies, waits for them, and re-layouts: 34.5 us -> none  [the longest x4 28 us: split_blocks(): piece.reshape(piece_rows // block_size, block_size, piece.shape[1] // HD,...]
    unnamed x18 -> x0, local copies, waits for them, and re-layouts: 33.6 us -> none
    all_to_all x5 -> x0, starting transfers between devices: 28.1 us -> none  [the longest x1 6.15 us: on_device(): lax.all_to_all(tangent_out, 'uly', split_axis=0, concat_axis=1, tiled=True)]
    all_to_all x10 -> x0, local copies, waits for them, and re-layouts: 14.5 us -> none  [the longest x2 3.4 us: on_device(): lax.all_to_all(mixed_out, 'uly', split_axis=0, concat_axis=1, tiled=True)]
  transfers between devices with their start and end apart: 9 -> 0, of which waited for: 5 -> 0; matrix products, arithmetic and copies ran while one was open for 34% -> 0% of each run, Pallas kernels for 0% -> 0%
where the time goes in v1:
time: 91.1 us; the launch traced here: 90.1 us
  Pallas kernels  86.1 us (95%)
  local copies, waits for them, and re-layouts  3.37 us (4%)
    pallas_call x1, Pallas kernels, on_device(): pl.pallas_call(kernel, out_shape=jax.ShapeDtypeStruct((2, QROWS, COLS), j...  86.1 us
    squeeze x1, local copies, waits for them, and re-layouts, on_device(): return (out[0], out[1])  3.37 us

profile of v1, /device:TPU:4, one launch (start us, length us, event | category | flops | bytes accessed | tf_op | source)
XLA Modules:
  0.0 90.1 jit_solution(6050504007253590651)
XLA Ops:
  0.6 86.1 %tangent_attention.1 = bf16[2,128,5120]{2,1,0:T(8,128)(2,1)} custom-call(bf16[128,5120]{1,0:T(8,128)(2,1)} %q_ref.1, bf16[16,5120]{1,0:T(8,128)(2,1)} %k_ref.1, bf16[16,5120]{1,0:T(8,128)(2,1)} %v_ref.1, bf16[128,5120]{1,0:T(8,128)(2,1)} %dq_ref.1, bf16[16,5120]{1,0:T(8,128)(2,1)} %dk_ref.1, bf16[16,5120]{1,0:T(8,128)(2,1)} %dv_ref.1), custom_call_target="tpu_custom_call" | custom-call | flops 16000000000 | bytes 6000000 | tf_op jit(solution)/shard_map/tangent_attention/pallas_call | solution.py:237
  86.8 3.4 %slice_bitcast_fusion = (bf16[128,5120]{1,0:T(8,128)(2,1)}, bf16[128,5120]{1,0:T(8,128)(2,1)}) fusion(bf16[2,128,5120]{2,1,0:T(8,128)(2,1)} %tangent_attention.1), kind=kLoop, calls=%fused_computation | loop fusion | bytes 5242880 | tf_op jit(solution)/shard_map/squeeze | solution.py:264

commit v2 on v1

--- a/solution.py
+++ b/solution.py
@@ -22,7 +22,22 @@
 SCALE_LOG2 = SCALE * math.log2(math.e)
 MESH = pl.DeviceIdType.MESH
 
-LAYOUT = ((0, 1, 2, 0),) * SLOTS
+LAYOUT = (
+    (0, 1, 2, 0),
+    (1, 2, 0, 0),
+    (2, 0, 1, 0),
+    (0, 1, 2, 1),
+    (1, 2, 0, 1),
+)
+
+PLAN = (
+    (" ".join(("keys0 keys1 keys2 keys3", "keys4 queries0 own0 own1", "own2 own3 own4 cross0", "cross1 near0 cross2 cross3", "near1 cross4 far0 near2", "near3 far1")),),
+    ("queries1 ready0", "near4", "queries2 far2", "far3",),
+    ("queries3 ready1", "far4", "queries4", "",),
+    ("ready2", "", "", "",),
+    ("ready3", "", "", "",),
+    ("ready4", "", "", "",),
+)
 
 
 def scores_of(left, right):
@@ -144,35 +159,62 @@
         ref = block_ref(slot, block)
         send(ref, ref, k2_send.at[slot], twin_recv.at[slot], places[slot].twin())
 
-    def along_all(slot, block, which):
+    def along(slot, block, which, step):
         ref = block_ref(slot, block)
-        for step in (1, 3, 2):
-            send(ref, ref, k2_send.at[slot], along_recv.at[slot, which, step - 1], places[slot].along(step))
-        to_twin(slot, block)
-
-    def own_block(slot):
+        hop = (1, 3)[which] if step == 2 else step
+        send(ref, ref, k2_send.at[slot], along_recv.at[slot, which, step - 1], places[slot].along(hop))
+
+    def own(slot):
         place = places[slot]
         ref = block_ref(slot, place.block)
         wait_bytes(ref, k1_recv.at[slot])
         send(ref, ref, k2_send.at[slot], across_recv.at[slot], place.across())
-        along_all(slot, place.block, 0)
-
-    def across_block(slot):
+        along(slot, place.block, 0, 1)
+        along(slot, place.block, 0, 3)
+        to_twin(slot, place.block)
+
+    def cross(slot):
         place = places[slot]
         block = place.block_of(3 - place.b, place.c, core)
         wait_bytes(block_ref(slot, block), across_recv.at[slot])
-        along_all(slot, block, 1)
-
-    def along_blocks(slot, which):
+        along(slot, block, 1, 3)
+        along(slot, block, 1, 1)
+        to_twin(slot, block)
+
+    def arrived(slot, which, step):
         place = places[slot]
         b = 3 - place.b if which else place.b
-        for step in (1, 3, 2):
-            block = place.block_of(b, lax.rem(place.c + 4 - step, 4), core)
-            wait_bytes(block_ref(slot, block), along_recv.at[slot, which, step - 1])
-            to_twin(slot, block)
+        block = place.block_of(b, lax.rem(place.c + 4 - step, 4), core)
+        wait_bytes(block_ref(slot, block), along_recv.at[slot, which, step - 1])
+        if step == (1, 3)[which]:
+            along(slot, block, which, 2)
+        to_twin(slot, block)
+
+    def near(slot):
+        arrived(slot, 0, 1)
+        arrived(slot, 0, 3)
+        arrived(slot, 1, 3)
+        arrived(slot, 1, 1)
+
+    def far(slot):
+        arrived(slot, 0, 2)
+        arrived(slot, 1, 2)
+
+    def ready(slot):
+        wait_bytes(k_all.at[slot, :, : KEYS // 2, :], twin_recv.at[slot])
+        wait_bytes(q_all.at[slot], q_recv.at[slot])
+
+    steps = {"keys": send_keys, "queries": send_queries, "own": own, "cross": cross, "near": near, "far": far, "ready": ready}
+
+    def follow(plan):
+        for step in plan.split():
+            steps[step[:-1]](int(step[-1]))
 
     def attend(slot):
         def tile(at, _):
+            for point in range(1, QUERIES // TILE):
+                if PLAN[slot + 1][point]:
+                    pl.when(at == point)(functools.partial(follow, PLAN[slot + 1][point]))
             here = rows(at * TILE, TILE)
             query, dquery = q_all[slot, 0, here, :], q_all[slot, 1, here, :]
             key, dkey = k_all[slot, 0], k_all[slot, 1]
@@ -184,45 +226,36 @@
             total = jnp.sum(weights, axis=1, keepdims=True)
             weights_rounded = weights.astype(jnp.bfloat16)
             product = weights * (tangents * SCALE)
-            moment = jnp.sum(product, axis=1, keepdims=True)
             both = mix(weights_rounded, jnp.concatenate([value, dvalue], 1))
             mixed = both[:, :HD] / total
-            tangent = (mix(product.astype(jnp.bfloat16), value) + both[:, HD:] - mixed * moment) / total
+            summed = mix(product.astype(jnp.bfloat16), jnp.concatenate([value, jnp.ones_like(value)], 1))
+            tangent = (summed[:, :HD] + both[:, HD:] - mixed * summed[:, HD:]) / total
             o_all[slot, 0, here, :] = mixed.astype(jnp.bfloat16)
             o_all[slot, 1, here, :] = tangent.astype(jnp.bfloat16)
+            send_outputs(slot, at)
             return 0
 
         lax.fori_loop(0, QUERIES // TILE, tile, 0)
 
-    def send_outputs(slot):
+    def send_outputs(slot, at):
         place = places[slot]
         there = out_ref.at[:, :, columns(slot * GROUP + place.kind)]
-        for device, member, _ in place.peers():
-            send(o_all.at[slot, :, rows(member * QROWS, QROWS), :], there, o_send.at[slot], o_recv, device)
-        pltpu.make_async_copy(o_all.at[slot, :, rows(place.member * QROWS, QROWS), :], there, o_recv).start()
-
+        for member in [at * (TILE // QROWS) + part for part in range(TILE // QROWS)]:
+            here = o_all.at[slot, :, rows(member * QROWS, QROWS), :]
+            device = place.device(lax.rem(member, 4), lax.div(place.b, 2) * 2 + lax.div(member, 4), place.c, core)
+
+            @pl.when(member != place.member)
+            def _():
+                send(here, there, o_send.at[slot], o_recv, device)
+
+            @pl.when(member == place.member)
+            def _():
+                pltpu.make_async_copy(here, there, o_recv).start()
+
+    follow(PLAN[0][0])
     for slot in range(SLOTS):
-        send_keys(slot)
-    send_queries(0)
-    own_block(0)
-    across_block(0)
-    send_queries(1)
-    own_block(1)
-    along_blocks(0, 0)
-    along_blocks(0, 1)
-    for slot in range(SLOTS):
-        if slot + 1 < SLOTS:
-            across_block(slot + 1)
-        if slot + 2 < SLOTS:
-            send_queries(slot + 2)
-            own_block(slot + 2)
-        wait_bytes(k_all.at[slot, :, : KEYS // 2, :], twin_recv.at[slot])
-        wait_bytes(q_all.at[slot], q_recv.at[slot])
+        follow(PLAN[slot + 1][0])
         attend(slot)
-        send_outputs(slot)
-        if slot + 1 < SLOTS:
-            along_blocks(slot + 1, 0)
-            along_blocks(slot + 1, 1)
 
     for slot in range(SLOTS):
         wait_bytes(k_all.at[slot, :, : 7 * KROWS, :], k1_send.at[slot])

time: 91.1 us -> 82 us (0.900)
  Pallas kernels: 86.1 us -> 77 us
    pallas_call x1, Pallas kernels: 86.1 us -> 77 us  [on_device(): pl.pallas_call(kernel, out_shape=jax.ShapeDtypeStruct((2, QROWS, COLS), j...]
where the time goes in v2:
time: 82 us; the launch traced here: 81 us
  Pallas kernels  77 us (94%)
  local copies, waits for them, and re-layouts  3.37 us (4%)
    pallas_call x1, Pallas kernels, on_device(): pl.pallas_call(kernel, out_shape=jax.ShapeDtypeStruct((2, QROWS, COLS), j...  77 us
    squeeze x1, local copies, waits for them, and re-layouts, on_device(): return (out[0], out[1])  3.37 us

profile of v2, /device:TPU:4, one launch (start us, length us, event | category | flops | bytes accessed | tf_op | source)
XLA Modules:
  0.0 81.0 jit_solution(2816167664225807843)
XLA Ops:
  0.6 77.0 %tangent_attention.1 = bf16[2,128,5120]{2,1,0:T(8,128)(2,1)} custom-call(bf16[128,5120]{1,0:T(8,128)(2,1)} %q_ref.1, bf16[16,5120]{1,0:T(8,128)(2,1)} %k_ref.1, bf16[16,5120]{1,0:T(8,128)(2,1)} %v_ref.1, bf16[128,5120]{1,0:T(8,128)(2,1)} %dq_ref.1, bf16[16,5120]{1,0:T(8,128)(2,1)} %dk_ref.1, bf16[16,5120]{1,0:T(8,128)(2,1)} %dv_ref.1), custom_call_target="tpu_custom_call" | custom-call | flops 16000000000 | bytes 6000000 | tf_op jit(solution)/shard_map/tangent_attention/pallas_call | solution.py:270
  77.6 3.4 %slice_bitcast_fusion = (bf16[128,5120]{1,0:T(8,128)(2,1)}, bf16[128,5120]{1,0:T(8,128)(2,1)}) fusion(bf16[2,128,5120]{2,1,0:T(8,128)(2,1)} %tangent_attention.1), kind=kLoop, calls=%fused_computation | loop fusion | bytes 5242880 | tf_op jit(solution)/shard_map/squeeze | solution.py:297

commit v3 on v2

--- a/solution.py
+++ b/solution.py
@@ -23,11 +23,11 @@
 MESH = pl.DeviceIdType.MESH
 
 LAYOUT = (
+    (2, 0, 1, 0),
+    (1, 2, 0, 0),
     (0, 1, 2, 0),
-    (1, 2, 0, 0),
-    (2, 0, 1, 0),
+    (1, 2, 0, 1),
     (0, 1, 2, 1),
-    (1, 2, 0, 1),
 )
 
 PLAN = (

time: 82 us -> 81.3 us (level); the launches traced: 81 us -> 81.2 us
  no operation moved by 1% of the time
where the time goes in v3:
time: 81.3 us; the launch traced here: 81.2 us
  Pallas kernels  77.1 us (95%)
  local copies, waits for them, and re-layouts  3.37 us (4%)
    pallas_call x1, Pallas kernels, on_device(): pl.pallas_call(kernel, out_shape=jax.ShapeDtypeStruct((2, QROWS, COLS), j...  77.1 us
    squeeze x1, local copies, waits for them, and re-layouts, on_device(): return (out[0], out[1])  3.37 us

profile of v3, /device:TPU:4, one launch (start us, length us, event | category | flops | bytes accessed | tf_op | source)
XLA Modules:
  0.0 81.2 jit_solution(11062811609521571309)
XLA Ops:
  0.6 77.1 %tangent_attention.1 = bf16[2,128,5120]{2,1,0:T(8,128)(2,1)} custom-call(bf16[128,5120]{1,0:T(8,128)(2,1)} %q_ref.1, bf16[16,5120]{1,0:T(8,128)(2,1)} %k_ref.1, bf16[16,5120]{1,0:T(8,128)(2,1)} %v_ref.1, bf16[128,5120]{1,0:T(8,128)(2,1)} %dq_ref.1, bf16[16,5120]{1,0:T(8,128)(2,1)} %dk_ref.1, bf16[16,5120]{1,0:T(8,128)(2,1)} %dv_ref.1), custom_call_target="tpu_custom_call" | custom-call | flops 16000000000 | bytes 6000000 | tf_op jit(solution)/shard_map/tangent_attention/pallas_call | solution.py:270
  77.8 3.4 %slice_bitcast_fusion = (bf16[128,5120]{1,0:T(8,128)(2,1)}, bf16[128,5120]{1,0:T(8,128)(2,1)}) fusion(bf16[2,128,5120]{2,1,0:T(8,128)(2,1)} %tangent_attention.1), kind=kLoop, calls=%fused_computation | loop fusion | bytes 5242880 | tf_op jit(solution)/shard_map/squeeze | solution.py:297

commit v4 on v3

--- a/solution.py
+++ b/solution.py
@@ -31,7 +31,10 @@
 )
 
 PLAN = (
-    (" ".join(("keys0 keys1 keys2 keys3", "keys4 queries0 own0 own1", "own2 own3 own4 cross0", "cross1 near0 cross2 cross3", "near1 cross4 far0 near2", "near3 far1")),),
+    (
+        " ".join(("keys0 keys1 keys2", "keys3 keys4")),
+        " ".join(("queries0 own0 own1 own2", "own3 own4 cross0 cross1", "near0 cross2 cross3 near1", "cross4 far0 near2 near3", "far1")),
+    ),
     ("queries1 ready0", "near4", "queries2 far2", "far3",),
     ("queries3 ready1", "far4", "queries4", "",),
     ("ready2", "", "", "",),
@@ -135,7 +138,7 @@
     for device in partners:
         pl.semaphore_signal(barrier, inc=1, device_id=device, device_id_type=MESH)
     pl.semaphore_wait(barrier, len(partners))
-    for copy in staged:
+    for copy in staged[:4]:
         copy.wait()
 
     def send_keys(slot):
@@ -253,6 +256,9 @@
                 pltpu.make_async_copy(here, there, o_recv).start()
 
     follow(PLAN[0][0])
+    for copy in staged[4:]:
+        copy.wait()
+    follow(PLAN[0][1])
     for slot in range(SLOTS):
         follow(PLAN[slot + 1][0])
         attend(slot)

time: 81.3 us -> 81.3 us (level)
  no operation moved by 1% of the time
where the time goes in v4:
time: 81.3 us; the launch traced here: 81.2 us
  Pallas kernels  77.2 us (95%)
  local copies, waits for them, and re-layouts  3.37 us (4%)
    pallas_call x1, Pallas kernels, on_device(): pl.pallas_call(kernel, out_shape=jax.ShapeDtypeStruct((2, QROWS, COLS), j...  77.2 us
    squeeze x1, local copies, waits for them, and re-layouts, on_device(): return (out[0], out[1])  3.37 us

profile of v4, /device:TPU:4, one launch (start us, length us, event | category | flops | bytes accessed | tf_op | source)
XLA Modules:
  0.0 81.2 jit_solution(14527000815551301695)
XLA Ops:
  0.6 77.2 %tangent_attention.1 = bf16[2,128,5120]{2,1,0:T(8,128)(2,1)} custom-call(bf16[128,5120]{1,0:T(8,128)(2,1)} %q_ref.1, bf16[16,5120]{1,0:T(8,128)(2,1)} %k_ref.1, bf16[16,5120]{1,0:T(8,128)(2,1)} %v_ref.1, bf16[128,5120]{1,0:T(8,128)(2,1)} %dq_ref.1, bf16[16,5120]{1,0:T(8,128)(2,1)} %dk_ref.1, bf16[16,5120]{1,0:T(8,128)(2,1)} %dv_ref.1), custom_call_target="tpu_custom_call" | custom-call | flops 16000000000 | bytes 6000000 | tf_op jit(solution)/shard_map/tangent_attention/pallas_call | solution.py:276
  77.8 3.4 %slice_bitcast_fusion = (bf16[128,5120]{1,0:T(8,128)(2,1)}, bf16[128,5120]{1,0:T(8,128)(2,1)}) fusion(bf16[2,128,5120]{2,1,0:T(8,128)(2,1)} %tangent_attention.1), kind=kLoop, calls=%fused_computation | loop fusion | bytes 5242880 | tf_op jit(solution)/shard_map/squeeze | solution.py:303
